TPU v7x, 32 devices: a whole 2x2x4 slice. The times are simulated.
32 devices in a mesh: clips: 2 (over x), rows: 16 (over z, y, core).
Axes of the slice: x: 2, y: 2, z: 4, core: 2. Of those that a mesh axis runs over, the one named last changes fastest.
Arguments:
- latents: bfloat16 [8, 64, 160, 384], P('clips', 'rows'), parts along dimension 0, may hold values from -6 to 6
- gamma: float32 [384], replicated, may hold values from 0.5 to 1.5
- weight: bfloat16 [3, 3, 3, 384, 384], replicated, may hold values from -0.0625 to 0.0625
- bias: float32 [384], replicated, may hold values from -3 to 3
- intersection: int32 [32], P('clips'), parts along dimension 0, may hold values from 0 to 2
- ramp: int32 [32], P('clips'), parts along dimension 0, may hold values from 1 to 3
Outputs:
- decoded: bfloat16 [8, 64, 160, 384], P('clips', 'rows'), parts along dimension 0
There are 2 independent parts, one for each index of `clips`. A program takes and returns all parts, laid end to end along the dimension named above; an argument that names none is the same for every part. Nothing has to cross between parts.
All inputs are finite; a program needn't handle non-finite values.
Results may differ from a plain program's by a relative error of at most 0.0034.
Values may be sent and summed in bfloat16 or wider, within the bound.
A program may use at most 448 MiB of HBM per device.

v0:
```python
import jax
import jax.numpy as jnp
from jax import lax
from jax.sharding import PartitionSpec as P

OV_MAX = 2


def shifted(block, axis, distance):
    devices = range(lax.axis_size(axis))
    route = [(i - distance, i) for i in devices if i - distance in devices]
    return lax.ppermute(block, axis, route)


def activate(tile, gamma, keep):
    values = tile.astype(jnp.float32)
    square = jnp.mean(values * values, axis=-1, keepdims=True)
    normed = values * lax.rsqrt(square + 1e-06) * gamma
    return (jax.nn.silu(normed) * keep).astype(jnp.bfloat16)


def convolve(stacked, weight, bias, count):
    padded = jnp.pad(stacked, ((0, 0), (1, 1), (1, 1), (0, 0)))
    height = stacked.shape[1]
    width = stacked.shape[2]
    total = jnp.zeros((count, height, width, weight.shape[4]), jnp.float32)
    for step_t in range(3):
        for step_h in range(3):
            for step_w in range(3):
                slab = padded[
                    step_t : step_t + count, step_h : step_h + height, step_w : step_w + width
                ]
                total = total + jnp.einsum(
                    "fhwc,cd->fhwd",
                    slab,
                    weight[step_t, step_h, step_w],
                    preferred_element_type=jnp.float32,
                )
    return total + bias


def per_device(latents, gamma, weight, bias, intersection, ramp):
    frames = latents.shape[0]
    rows = latents.shape[1]
    extra = OV_MAX
    index = lax.axis_index("rows")
    count = lax.axis_size("rows")
    own_ov = jnp.where(index == count - 1, 0, intersection[index])
    previous = jnp.maximum(index - 1, 0)
    prev_ov = jnp.where(index > 0, intersection[previous], 0)
    prev_ramp = ramp[previous]
    places = jnp.arange(rows + extra, dtype=jnp.int32)
    keep = (places < rows + own_ov).astype(jnp.float32).reshape(1, -1, 1, 1)
    offsets = jnp.arange(extra, dtype=jnp.int32)
    blend_w = jnp.where(
        offsets < prev_ov,
        jnp.maximum(prev_ramp - offsets, 0).astype(jnp.float32)
        / (prev_ramp + 1).astype(jnp.float32),
        jnp.float32(0.0),
    )
    blend_w = blend_w.reshape(1, -1, 1, 1)
    width = latents.shape[2]
    chans = latents.shape[3]
    below = shifted(latents, "rows", -1)
    tile = jnp.concatenate([latents, below[:, :extra]], axis=1)
    start = jnp.zeros((2, rows + extra, width, chans), jnp.bfloat16)
    act = activate(tile, gamma, keep)
    stacked = jnp.concatenate([start, act], axis=0)
    outcome = (tile.astype(jnp.float32) + convolve(stacked, weight, bias, frames)).astype(
        jnp.bfloat16
    )
    outcome, unused = (outcome, stacked[frames:])
    arrived = shifted(outcome[:, rows:], "rows", 1)
    own_rows = outcome[:, :rows]
    head = own_rows[:, :extra].astype(jnp.float32)
    mixed = blend_w * arrived.astype(jnp.float32) + (1.0 - blend_w) * head
    return jnp.concatenate([mixed.astype(jnp.bfloat16), own_rows[:, extra:]], axis=1)


def solution(mesh):
    in_specs = (P("clips", "rows", None, None), P(), P(), P(), P("clips"), P("clips"))
    out_specs = P("clips", "rows", None, None)
    return jax.shard_map(
        per_device, mesh=mesh, in_specs=in_specs, out_specs=out_specs, check_vma=False
    )
```

profile of v0, /device:TPU:1, one launch (start us, length us, event | category | flops | bytes accessed | tf_op | source)
XLA Modules:
  0.0 218.2 jit_solution(15525754383371504543)
XLA Ops:
  4.0 23.0 %collective-permute-done = bf16[4,4,160,384]{3,2,1,0:T(8,128)(2,1)S(1)} collective-permute-done((bf16[4,4,160,384]{3,2,1,0:T(8,128)(2,1)}, bf16[4,4,160,384]{3,2,1,0:T(8,128)(2,1)S(1)}, u32[]{:S(2)}, u32[]{:S(2)}) %collective-permute-start) | collective-permute-done | bytes 1966112 | tf_op jit(solution)/shard_map/ppermute | solution.py:12
  34.1 4.5 %fusion.11 = f32[4,6,160,384]{3,2,1,0:T(8,128)} fusion(bf16[4,6,160,384]{3,2,1,0:T(8,128)(2,1)S(1)} %fusion.8, bf16[3,3,3,384,384]{4,3,2,1,0:T(8,128)(2,1)S(1)} %copy-done.2), kind=kOutput, calls=%fused_computation.38 | convolution fusion | flops 1132462080 | bytes 9142272 | tf_op jit(solution)/shard_map/fhwc,cd->fhwd/dot_general | solution.py:33
  43.0 4.5 %fusion.13 = f32[4,6,160,384]{3,2,1,0:T(8,128)} fusion(bf16[4,6,160,384]{3,2,1,0:T(8,128)(2,1)S(1)} %fusion.8, bf16[3,3,3,384,384]{4,3,2,1,0:T(8,128)(2,1)S(1)} %copy-done.2), kind=kOutput, calls=%fused_computation.40 | convolution fusion | flops 1132462080 | bytes 9142272 | tf_op jit(solution)/shard_map/fhwc,cd->fhwd/dot_general | solution.py:33
  47.4 4.4 %fusion.14 = f32[4,6,160,384]{3,2,1,0:T(8,128)} fusion(bf16[4,6,160,384]{3,2,1,0:T(8,128)(2,1)S(1)} %fusion.8, bf16[3,3,3,384,384]{4,3,2,1,0:T(8,128)(2,1)S(1)} %copy-done.2), kind=kOutput, calls=%fused_computation.41 | convolution fusion | flops 1132462080 | bytes 9142272 | tf_op jit(solution)/shard_map/fhwc,cd->fhwd/dot_general | solution.py:33
  56.3 4.4 %fusion.16 = f32[4,6,160,384]{3,2,1,0:T(8,128)} fusion(bf16[4,6,160,384]{3,2,1,0:T(8,128)(2,1)S(1)} %fusion.8, bf16[3,3,3,384,384]{4,3,2,1,0:T(8,128)(2,1)S(1)} %copy-done.2), kind=kOutput, calls=%fused_computation.43 | convolution fusion | flops 1132462080 | bytes 9142272 | tf_op jit(solution)/shard_map/fhwc,cd->fhwd/dot_general | solution.py:33
  60.7 4.6 %fusion.17 = f32[4,6,160,384]{3,2,1,0:T(8,128)} fusion(bf16[4,6,160,384]{3,2,1,0:T(8,128)(2,1)S(1)} %fusion.8, bf16[3,3,3,384,384]{4,3,2,1,0:T(8,128)(2,1)S(1)} %copy-done.2), kind=kOutput, calls=%fused_computation.44 | convolution fusion | flops 1132462080 | bytes 9142272 | tf_op jit(solution)/shard_map/fhwc,cd->fhwd/dot_general | solution.py:33
  65.4 4.4 %fusion.18 = f32[4,6,160,384]{3,2,1,0:T(8,128)} fusion(bf16[4,6,160,384]{3,2,1,0:T(8,128)(2,1)S(1)} %fusion.8, bf16[3,3,3,384,384]{4,3,2,1,0:T(8,128)(2,1)S(1)} %copy-done.2), kind=kOutput, calls=%fused_computation.45 | convolution fusion | flops 1132462080 | bytes 9142272 | tf_op jit(solution)/shard_map/fhwc,cd->fhwd/dot_general | solution.py:33
  69.8 4.5 %fusion.19 = f32[4,6,160,384]{3,2,1,0:T(8,128)} fusion(bf16[4,6,160,384]{3,2,1,0:T(8,128)(2,1)S(1)} %fusion.8, bf16[3,3,3,384,384]{4,3,2,1,0:T(8,128)(2,1)S(1)} %copy-done.2), kind=kOutput, calls=%fused_computation.46 | convolution fusion | flops 1132462080 | bytes 9142272 | tf_op jit(solution)/shard_map/fhwc,cd->fhwd/dot_general | solution.py:33
  74.3 4.4 %fusion.20 = f32[4,6,160,384]{3,2,1,0:T(8,128)} fusion(bf16[4,6,160,384]{3,2,1,0:T(8,128)(2,1)S(1)} %fusion.8, bf16[3,3,3,384,384]{4,3,2,1,0:T(8,128)(2,1)S(1)} %copy-done.2), kind=kOutput, calls=%fused_computation.47 | convolution fusion | flops 1132462080 | bytes 9142272 | tf_op jit(solution)/shard_map/fhwc,cd->fhwd/dot_general | solution.py:33
  78.7 4.4 %fusion.21 = f32[4,6,160,384]{3,2,1,0:T(8,128)} fusion(bf16[4,6,160,384]{3,2,1,0:T(8,128)(2,1)S(1)} %fusion.8, bf16[3,3,3,384,384]{4,3,2,1,0:T(8,128)(2,1)S(1)} %copy-done.2), kind=kOutput, calls=%fused_computation.48 | convolution fusion | flops 1132462080 | bytes 9142272 | tf_op jit(solution)/shard_map/fhwc,cd->fhwd/dot_general | solution.py:33
  83.1 4.6 %fusion.22 = f32[4,6,160,384]{3,2,1,0:T(8,128)} fusion(bf16[4,6,160,384]{3,2,1,0:T(8,128)(2,1)S(1)} %fusion.8, bf16[3,3,3,384,384]{4,3,2,1,0:T(8,128)(2,1)S(1)} %copy-done.2), kind=kOutput, calls=%fused_computation.49 | convolution fusion | flops 1132462080 | bytes 9142272 | tf_op jit(solution)/shard_map/fhwc,cd->fhwd/dot_general | solution.py:33
  87.7 4.6 %fusion.23 = f32[4,6,160,384]{3,2,1,0:T(8,128)} fusion(bf16[4,6,160,384]{3,2,1,0:T(8,128)(2,1)S(1)} %fusion.8, bf16[3,3,3,384,384]{4,3,2,1,0:T(8,128)(2,1)S(1)} %copy-done.2), kind=kOutput, calls=%fused_computation.50 | convolution fusion | flops 1132462080 | bytes 9142272 | tf_op jit(solution)/shard_map/fhwc,cd->fhwd/dot_general | solution.py:33
  92.4 4.6 %fusion.24 = f32[4,6,160,384]{3,2,1,0:T(8,128)} fusion(bf16[4,6,160,384]{3,2,1,0:T(8,128)(2,1)S(1)} %fusion.8, bf16[3,3,3,384,384]{4,3,2,1,0:T(8,128)(2,1)S(1)} %copy-done.2), kind=kOutput, calls=%fused_computation.51 | convolution fusion | flops 1132462080 | bytes 9142272 | tf_op jit(solution)/shard_map/fhwc,cd->fhwd/dot_general | solution.py:33
  96.9 4.5 %fusion.25 = f32[4,6,160,384]{3,2,1,0:T(8,128)} fusion(bf16[4,6,160,384]{3,2,1,0:T(8,128)(2,1)S(1)} %fusion.8, bf16[3,3,3,384,384]{4,3,2,1,0:T(8,128)(2,1)S(1)} %copy-done.2), kind=kOutput, calls=%fused_computation.52 | convolution fusion | flops 1132462080 | bytes 9142272 | tf_op jit(solution)/shard_map/fhwc,cd->fhwd/dot_general | solution.py:33
  105.8 4.5 %fusion.27 = f32[4,6,160,384]{3,2,1,0:T(8,128)} fusion(bf16[4,6,160,384]{3,2,1,0:T(8,128)(2,1)S(1)} %fusion.8, bf16[3,3,3,384,384]{4,3,2,1,0:T(8,128)(2,1)S(1)} %copy-done.2), kind=kOutput, calls=%fused_computation.54 | convolution fusion | flops 1132462080 | bytes 9142272 | tf_op jit(solution)/shard_map/fhwc,cd->fhwd/dot_general | solution.py:33
  114.7 4.9 %fusion.29 = f32[4,6,160,384]{3,2,1,0:T(8,128)} fusion(bf16[4,6,160,384]{3,2,1,0:T(8,128)(2,1)S(1)} %fusion.8, bf16[3,3,3,384,384]{4,3,2,1,0:T(8,128)(2,1)S(1)} %copy-done.2), kind=kOutput, calls=%fused_computation.56 | convolution fusion | flops 1132462080 | bytes 9142272 | tf_op jit(solution)/shard_map/fhwc,cd->fhwd/dot_general | solution.py:33
  124.0 4.5 %fusion.31 = f32[4,6,160,384]{3,2,1,0:T(8,128)} fusion(bf16[4,6,160,384]{3,2,1,0:T(8,128)(2,1)S(1)} %fusion.8, bf16[3,3,3,384,384]{4,3,2,1,0:T(8,128)(2,1)S(1)} %copy-done.2), kind=kOutput, calls=%fused_computation.58 | convolution fusion | flops 1132462080 | bytes 9142272 | tf_op jit(solution)/shard_map/fhwc,cd->fhwd/dot_general | solution.py:33
  128.5 4.5 %fusion.32 = f32[4,6,160,384]{3,2,1,0:T(8,128)} fusion(bf16[4,6,160,384]{3,2,1,0:T(8,128)(2,1)S(1)} %fusion.8, bf16[3,3,3,384,384]{4,3,2,1,0:T(8,128)(2,1)S(1)} %copy-done.2), kind=kOutput, calls=%fused_computation.59 | convolution fusion | flops 1132462080 | bytes 9142272 | tf_op jit(solution)/shard_map/fhwc,cd->fhwd/dot_general | solution.py:33
  133.0 4.5 %fusion.33 = f32[4,6,160,384]{3,2,1,0:T(8,128)} fusion(bf16[4,6,160,384]{3,2,1,0:T(8,128)(2,1)S(1)} %fusion.8, bf16[3,3,3,384,384]{4,3,2,1,0:T(8,128)(2,1)S(1)} %copy-done.2), kind=kOutput, calls=%fused_computation.60 | convolution fusion | flops 1132462080 | bytes 9142272 | tf_op jit(solution)/shard_map/fhwc,cd->fhwd/dot_general | solution.py:33
  137.5 4.5 %fusion.48 = f32[4,6,160,384]{3,2,1,0:T(8,128)} fusion(bf16[4,6,160,384]{3,2,1,0:T(8,128)(2,1)S(1)} %fusion.8, bf16[3,3,3,384,384]{4,3,2,1,0:T(8,128)(2,1)S(1)} %copy-done.2), kind=kOutput, calls=%fused_computation.78 | convolution fusion | flops 849346560 | bytes 9142272 | tf_op jit(solution)/shard_map/fhwc,cd->fhwd/dot_general | solution.py:33
  141.9 4.6 %fusion.58 = f32[4,6,160,384]{3,2,1,0:T(8,128)} fusion(bf16[4,6,160,384]{3,2,1,0:T(8,128)(2,1)S(1)} %fusion.8, bf16[3,3,3,384,384]{4,3,2,1,0:T(8,128)(2,1)S(1)} %copy-done.2), kind=kOutput, calls=%fused_computation.88 | convolution fusion | flops 566231040 | bytes 9142272 | tf_op jit(solution)/shard_map/fhwc,cd->fhwd/dot_general | solution.py:33
  146.6 4.5 %fusion.38 = f32[4,6,160,384]{3,2,1,0:T(8,128)} fusion(bf16[4,6,160,384]{3,2,1,0:T(8,128)(2,1)S(1)} %fusion.8, bf16[3,3,3,384,384]{4,3,2,1,0:T(8,128)(2,1)S(1)} %copy-done.2), kind=kOutput, calls=%fused_computation.68 | convolution fusion | flops 1132462080 | bytes 9142272 | tf_op jit(solution)/shard_map/fhwc,cd->fhwd/dot_general | solution.py:33
  151.0 49.2 %fusion.9 = bf16[4,6,160,384]{3,2,1,0:T(8,128)(2,1)} fusion(f32[4,6,160,384]{3,2,1,0:T(8,128)} %fusion.33, f32[4,6,160,384]{3,2,1,0:T(8,128)} %fusion.32, f32[4,6,160,384]{3,2,1,0:T(8,128)} %fusion.31, f32[4,6,160,384]{3,2,1,0:T(8,128)} %fusion.38, f32[4,6,160,384]{3,2,1,0:T(8,128)} %fusion.30, f32[4,6,160,384]{3,2,1,0:T(8,128)} %fusion.29, ...), kind=kOutput, calls=%fused_computation.36 | convolution fusion | flops 1178173440 | bytes 162498048 | tf_op jit(solution)/shard_map/fhwc,cd->fhwd/dot_general | solution.py:33
  206.4 8.5 %collective-permute-done.1 = bf16[4,2,160,384]{3,2,1,0:T(8,128)(2,1)S(1)} collective-permute-done((bf16[4,2,160,384]{3,2,1,0:T(8,128)(2,1)S(1)}, bf16[4,2,160,384]{3,2,1,0:T(8,128)(2,1)S(1)}, u32[]{:S(2)}, u32[]{:S(2)}) %collective-permute-start.1) | collective-permute-done | bytes 983072 | tf_op jit(solution)/shard_map/ppermute | solution.py:12
  (28 shorter events, 40.4 us)
Async XLA Ops:
  0.0 27.0 %collective-permute-start = (bf16[4,4,160,384]{3,2,1,0:T(8,128)(2,1)}, bf16[4,4,160,384]{3,2,1,0:T(8,128)(2,1)S(1)}, u32[]{:S(2)}, u32[]{:S(2)}) collective-permute-start(bf16[4,4,160,384]{3,2,1,0:T(8,128)(2,1)} %param.6), channel_id=1, source_target_pairs={{1,0},{2,1},{3,2},{4,3},{5,4},{6,5},{7,6},{8,7},{9,8},{10,9},{11,1... | collective-permute-start | bytes 5898248 | tf_op jit(solution)/shard_map/ppermute | solution.py:12
  4.0 26.0 %copy-start = (bf16[4,4,160,384]{3,2,1,0:T(8,128)(2,1)S(1)}, bf16[4,4,160,384]{3,2,1,0:T(8,128)(2,1)}, u32[]{:S(2)}) copy-start(bf16[4,4,160,384]{3,2,1,0:T(8,128)(2,1)} %param.6) | copy-start | bytes 5898244
  4.0 30.1 %copy-start.2 = (bf16[3,3,3,384,384]{4,3,2,1,0:T(8,128)(2,1)S(1)}, bf16[3,3,3,384,384]{4,3,2,1,0:T(8,128)(2,1)}, u32[]{:S(2)}) copy-start(bf16[3,3,3,384,384]{4,3,2,1,0:T(8,128)(2,1)} %param.8) | copy-start | bytes 23887876
  27.2 11.4 %copy-start.1 = (bf16[4,2,160,384]{3,2,1,0:T(8,128)(2,1)}, bf16[4,2,160,384]{3,2,1,0:T(8,128)(2,1)S(1)}, u32[]{:S(2)}) copy-start(bf16[4,2,160,384]{3,2,1,0:T(8,128)(2,1)S(1)} %slice.235) | copy-start | bytes 2949124
  146.5 4.5 %copy-start.3 = (f32[384]{0:T(512)S(1)}, f32[384]{0:T(512)}, u32[]{:S(2)}) copy-start(f32[384]{0:T(512)} %param.9) | copy-start | bytes 4612
  151.0 52.9 %copy-start.4 = (s32[16]{0:T(128)S(1)}, s32[16]{0:T(128)}, u32[]{:S(2)}) copy-start(s32[16]{0:T(128)} %param.11) | copy-start | bytes 196
  201.9 12.9 %collective-permute-start.1 = (bf16[4,2,160,384]{3,2,1,0:T(8,128)(2,1)S(1)}, bf16[4,2,160,384]{3,2,1,0:T(8,128)(2,1)S(1)}, u32[]{:S(2)}, u32[]{:S(2)}) collective-permute-start(bf16[4,2,160,384]{3,2,1,0:T(8,128)(2,1)S(1)} %get-tuple-element.7), channel_id=1, source_target_pairs={{0,1},{1,2},{2,3},{3,4},{4,5},{5,6},{6,7},{7,8},{8,9},{9,10},{10,1... | collective-permute-start | bytes 2949128 | tf_op jit(solution)/shard_map/ppermute | solution.py:12
where the time goes:
time: 222 us; the launch traced here: 218 us
  matrix products  166 us (75%)
  waiting for transfers between devices  31.5 us (14%)
  other arithmetic  10.7 us (5%)
  starting transfers between devices  3.88 us (2%)
  local copies, waits for them, and re-layouts  3.76 us (2%)
  between operations  2.28 us (1%)
    dot_general x27, matrix products, convolve(): jnp.einsum('fhwc,cd->fhwd', slab, weight[step_t, step_h, step_w], preferr...  166 us
    ppermute x2, waiting for transfers between devices, shifted(): return lax.ppermute(block, axis, route)  31.5 us
  transfers between devices with their start and end apart: 2, of which 2 were waited for; matrix products, arithmetic and copies ran while one was open for 1% of the time, Pallas kernels for 0%

commit v1 on v0

v1 whole, which is shorter than its diff:
```python
import functools

import jax
import jax.numpy as jnp
from jax import lax
from jax.experimental import pallas as pl
from jax.experimental.pallas import tpu as pltpu
from jax.sharding import PartitionSpec as P

TAPS = 3
STEP = 256
MESH = pl.DeviceIdType.MESH

ROW_OF = ((1, 2), (0, 3))


def kernel(
    frames, width, chans, count,
    x_ref, w_ref, gamma_ref, bias_ref, inter_ref, ramp_ref,
    out_ref,
    xbuf, top, bot, lhs, wbuf, acc, ost,
    xsem, wsem, osem, send_sem, recv_sem,
):
    me = lax.axis_index("rows")
    span = TAPS * chans
    last = xbuf.shape[1] - 1

    def x_copy(f):
        return pltpu.make_async_copy(x_ref.at[f], xbuf.at[f], xsem.at[f])

    def w_copy(t):
        return pltpu.make_async_copy(
            w_ref.at[TAPS - 1 - t], wbuf.at[:, pl.ds(t * chans, chans)], wsem.at[t]
        )

    down = pltpu.make_async_remote_copy(
        src_ref=x_ref.at[:, last], dst_ref=top, send_sem=send_sem.at[0],
        recv_sem=recv_sem.at[0], device_id={"rows": me + 1}, device_id_type=MESH,
    )
    up = pltpu.make_async_remote_copy(
        src_ref=x_ref.at[:, 0], dst_ref=bot, send_sem=send_sem.at[1],
        recv_sem=recv_sem.at[1], device_id={"rows": me - 1}, device_id_type=MESH,
    )

    for f in range(frames):
        x_copy(f).start()
    for t in range(TAPS):
        w_copy(t).start()

    barrier = pltpu.get_barrier_semaphore()

    @pl.when(me > 0)
    def _():
        pl.semaphore_signal(
            barrier, inc=1, device_id={"rows": me - 1}, device_id_type=MESH
        )

    @pl.when(me < count - 1)
    def _():
        pl.semaphore_signal(
            barrier, inc=1, device_id={"rows": me + 1}, device_id_type=MESH
        )

    peers = jnp.where(me > 0, 1, 0) + jnp.where(me < count - 1, 1, 0)
    pl.semaphore_wait(barrier, peers)

    @pl.when(me < count - 1)
    def _():
        down.start()

    @pl.when(me > 0)
    def _():
        up.start()

    before = jnp.maximum(me - 1, 0)
    prev_ov = jnp.where(me > 0, inter_ref[before], 0)
    own_ov = jnp.where(me == count - 1, 0, inter_ref[me])
    ovv = jnp.full((1, chans), prev_ov, jnp.int32)
    ownv = jnp.full((1, chans), own_ov, jnp.int32)
    rampv = jnp.full((1, chans), ramp_ref[before], jnp.int32).astype(jnp.float32)
    a0 = jnp.where(ovv > 0, jnp.maximum(rampv, 0.0) / (rampv + 1.0), 0.0)
    a1 = jnp.where(ovv > 1, jnp.maximum(rampv - 1.0, 0.0) / (rampv + 1.0), 0.0)
    s1 = jnp.where(ovv > 1, 1.0, 1.0 - a0)
    s2 = 1.0 - a1
    live = jnp.where(ownv > 0, 1.0, 0.0)
    gamma = gamma_ref[...]
    bias = bias_ref[...]
    columns = lax.broadcasted_iota(jnp.int32, (width, chans), 0)

    def activate(values):
        square = jnp.mean(values * values, axis=-1, keepdims=True)
        half = values * lax.rsqrt(square + 1e-06) * (0.5 * gamma)
        return half + half * jnp.tanh(half)

    def place(f, value, targets):
        left = jnp.where(columns == 0, 0.0, pltpu.roll(value, 1, 0))
        right = jnp.where(columns == width - 1, 0.0, pltpu.roll(value, width - 1, 0))
        for scale, spots in targets:
            for step_w, part in enumerate((left, value, right)):
                if scale is not None:
                    part = part * scale
                part = part.astype(jnp.bfloat16)
                for half, slot, step_h in spots:
                    lhs[
                        half, f, slot * width : (slot + 1) * width,
                        step_h * span + step_w * chans : step_h * span + (step_w + 1) * chans,
                    ] = part

    own_targets = (
        ((None, ((1, 0, 1), (0, 0, 0))),),
        ((None, ((0, 0, 1), (0, 1, 0))), (s1, ((1, 0, 2),))),
        ((None, ((0, 1, 1), (1, 1, 0))), (s2, ((0, 0, 2),))),
        ((None, ((0, 1, 2), (1, 1, 1))),),
    )
    home = ((1, 0), (0, 0), (0, 1), (1, 1))

    wbuf[:, TAPS * chans :] = jnp.zeros(
        (wbuf.shape[0], wbuf.shape[1] - TAPS * chans), wbuf.dtype
    )
    acc[:, :, frames * chans :] = jnp.zeros(
        (2, 2 * width, acc.shape[2] - frames * chans), acc.dtype
    )

    def own_frame(f, carry):
        x_copy(f).wait()
        at = pl.ds(pl.multiple_of(f * chans, 128), chans)
        for row in range(last + 1):
            values = xbuf[f, row].astype(jnp.float32)
            half, slot = home[row]
            acc[half, slot * width : (slot + 1) * width, at] = values + bias
            place(f, activate(values), own_targets[row])
        return carry

    lax.fori_loop(0, frames, own_frame, 0)

    def multiply(half, f, j):
        taken = pl.ds(pl.multiple_of(j * STEP, STEP), STEP)
        put = pl.ds(pl.multiple_of(f * chans + j * STEP, 128), STEP)
        acc[half, :, put] += jnp.dot(
            lhs[half, f], wbuf[:, taken], preferred_element_type=jnp.float32
        )

    def out_copy(half, f, slot):
        row = ROW_OF[half][slot]
        return pltpu.make_async_copy(
            ost.at[f, row], out_ref.at[f, row], osem.at[f, row]
        )

    def work(half):
        for f in range(frames):
            reach = min(TAPS, frames - f) * chans
            steps = -(-reach // STEP)

            def body(j, carry, f=f):
                multiply(half, f, j)
                return carry

            lax.fori_loop(0, steps, body, 0)
            for slot in range(2):
                ost[f, ROW_OF[half][slot]] = acc[
                    half, slot * width : (slot + 1) * width, f * chans : (f + 1) * chans
                ].astype(jnp.bfloat16)
                out_copy(half, f, slot).start()

    for t in range(TAPS):
        w_copy(t).wait()
    work(0)

    @pl.when(me > 0)
    def _():
        down.wait_recv()

    @pl.when(me == 0)
    def _():
        top[...] = jnp.zeros(top.shape, top.dtype)

    @pl.when(me < count - 1)
    def _():
        up.wait_recv()

    @pl.when(me == count - 1)
    def _():
        bot[...] = jnp.zeros(bot.shape, bot.dtype)

    def edge_frame(f, carry):
        place(f, activate(top[f].astype(jnp.float32)), ((a0, ((1, 0, 0),)),))
        place(f, activate(bot[f].astype(jnp.float32)), ((live, ((1, 1, 2),)),))
        return carry

    lax.fori_loop(0, frames, edge_frame, 0)
    work(1)

    for half in range(2):
        for f in range(frames):
            for slot in range(2):
                out_copy(half, f, slot).wait()

    @pl.when(me < count - 1)
    def _():
        down.wait_send()

    @pl.when(me > 0)
    def _():
        up.wait_send()


def per_device(latents, gamma, weight, bias, intersection, ramp):
    frames, rows, width, chans = latents.shape
    count = lax.axis_size("rows")
    taps = weight.reshape(TAPS, TAPS * TAPS * chans, chans)
    depth = taps.shape[1]
    wide = -(-TAPS * chans // STEP) * STEP
    total = (frames - 1) * chans + -(-chans // STEP) * STEP
    total = max(total, (frames - TAPS) * chans + wide)
    any_space = pl.BlockSpec(memory_space=pl.ANY)
    vmem = pl.BlockSpec(memory_space=pltpu.VMEM)
    smem = pl.BlockSpec(memory_space=pltpu.SMEM)
    return pl.pallas_call(
        functools.partial(kernel, frames, width, chans, count),
        out_shape=jax.ShapeDtypeStruct(latents.shape, latents.dtype),
        in_specs=[any_space, any_space, vmem, vmem, smem, smem],
        out_specs=any_space,
        scratch_shapes=[
            pltpu.VMEM((frames, rows, width, chans), jnp.bfloat16),
            pltpu.VMEM((frames, width, chans), jnp.bfloat16),
            pltpu.VMEM((frames, width, chans), jnp.bfloat16),
            pltpu.VMEM((2, frames, 2 * width, depth), jnp.bfloat16),
            pltpu.VMEM((depth, wide), jnp.bfloat16),
            pltpu.VMEM((2, 2 * width, total), jnp.float32),
            pltpu.VMEM((frames, rows, width, chans), jnp.bfloat16),
            pltpu.SemaphoreType.DMA((frames,)),
            pltpu.SemaphoreType.DMA((TAPS,)),
            pltpu.SemaphoreType.DMA((frames, rows)),
            pltpu.SemaphoreType.DMA((2,)),
            pltpu.SemaphoreType.DMA((2,)),
        ],
        compiler_params=pltpu.CompilerParams(
            collective_id=0, has_side_effects=True, vmem_limit_bytes=50 * 1024 * 1024
        ),
    )(latents, taps, gamma.reshape(1, chans), bias.reshape(1, chans), intersection, ramp)


def solution(mesh):
    in_specs = (P("clips", "rows", None, None), P(), P(), P(), P("clips"), P("clips"))
    out_specs = P("clips", "rows", None, None)
    return jax.shard_map(
        per_device, mesh=mesh, in_specs=in_specs, out_specs=out_specs, check_vma=False
    )
```

time: 222 us -> 40.3 us (0.18); the launches traced: 218 us -> 40.1 us
  matrix products: 166 us -> 0 us
  Pallas kernels: 0 us -> 34.6 us
  waiting for transfers between devices: 31.5 us -> 0 us
  other arithmetic: 10.7 us -> 0 us
  starting transfers between devices: 3.88 us -> 0 us
  between operations: 2.28 us -> 0.01 us
    dot_general x27 -> x0, matrix products: 166 us -> none  [convolve(): jnp.einsum('fhwc,cd->fhwd', slab, weight[step_t, step_h, step_w], preferr...]
    pallas_call x0 -> x1, Pallas kernels: none -> 34.6 us  [per_device(): pl.pallas_call(functools.partial(kernel, frames, width, chans, count), ou...]
    ppermute x2 -> x0, waiting for transfers between devices: 31.5 us -> none  [shifted(): return lax.ppermute(block, axis, route)]
    convert_element_type x3 -> x0, other arithmetic: 5.71 us -> none  [the longest x1 4.05 us: activate(): return (jax.nn.silu(normed) * keep).astype(jnp.bfloat16)]
    unnamed x10 -> x7, local copies, waits for them, and re-layouts: 0.03 us -> 4.13 us
    ppermute x2 -> x0, starting transfers between devices: 3.88 us -> none  [shifted(): return lax.ppermute(block, axis, route)]
    reduce_sum x1 -> x0, other arithmetic: 2.8 us -> none  [activate(): square = jnp.mean(values * values, axis=-1, keepdims=True)]
  transfers between devices with their start and end apart: 2 -> 0, of which waited for: 2 -> 0; matrix products, arithmetic and copies ran while one was open for 1% -> 0% of each run, Pallas kernels for 0% -> 0%
where the time goes in v1:
time: 40.3 us; the launch traced here: 40.1 us
  Pallas kernels  34.6 us (86%)
  local copies, waits for them, and re-layouts  5.49 us (14%)
    pallas_call x1, Pallas kernels, per_device(): pl.pallas_call(functools.partial(kernel, frames, width, chans, count), ou...  34.6 us
    unnamed x7, local copies, waits for them, and re-layouts  4.13 us

profile of v1, /device:TPU:1, one launch (start us, length us, event | category | flops | bytes accessed | tf_op | source)
XLA Modules:
  0.0 40.1 jit_solution(15666985934595510593)
XLA Ops:
  0.0 0.7 %reshape.10.gamma_ref = f32[1,384]{1,0:T(1,128)S(1)} reshape(f32[384]{0:T(512)} %param.7) | data formatting | bytes 3072 | tf_op jit(solution)/shard_map/reshape | solution.py:240
  0.7 0.7 %reshape.11.bias_ref = f32[1,384]{1,0:T(1,128)S(1)} reshape(f32[384]{0:T(512)} %param.9) | data formatting | bytes 3072 | tf_op jit(solution)/shard_map/reshape | solution.py:240
  1.4 0.0 copy-start
  1.4 1.5 %copy-done = bf16[4,4,160,384]{3,2,1,0:T(8,128)(2,1)S(1)} copy-done((bf16[4,4,160,384]{3,2,1,0:T(8,128)(2,1)S(1)}, bf16[4,4,160,384]{3,2,1,0:T(8,128)(2,1)}, u32[]{:S(2)}) %copy-start) | copy-done | bytes 1966104
  2.9 0.0 copy-start.1
  2.9 0.7 %copy-done.1 = s32[16]{0:T(128)S(1)} copy-done((s32[16]{0:T(128)S(1)}, s32[16]{0:T(128)}, u32[]{:S(2)}) %copy-start.1) | copy-done | bytes 88
  3.6 0.0 copy-start.2
  3.6 0.7 %copy-done.2 = s32[16]{0:T(128)S(1)} copy-done((s32[16]{0:T(128)S(1)}, s32[16]{0:T(128)}, u32[]{:S(2)}) %copy-start.2) | copy-done | bytes 88
  4.2 34.6 %shard_map.64 = bf16[4,4,160,384]{3,2,1,0:T(8,128)(2,1)S(1)} custom-call(bf16[4,4,160,384]{3,2,1,0:T(8,128)(2,1)S(1)} %copy-done, bf16[3,3456,384]{2,1,0:T(8,128)(2,1)} %bitcast.1, f32[1,384]{1,0:T(1,128)S(1)} %reshape.10.gamma_ref, f32[1,384]{1,0:T(1,128)S(1)} %reshape.11.bias_ref, s32[16]{0:T(128)S(1)} %copy-done.1, s32[16]{0:T(128)S(1)} %copy-done.2), custom_call_target="tpu_custom_call" | custom-call | tf_op jit(solution)/shard_map/pallas_call | solution.py:218
  38.9 1.3 %copy.8 = bf16[4,4,160,384]{3,2,1,0:T(8,128)(2,1)} copy(bf16[4,4,160,384]{3,2,1,0:T(8,128)(2,1)S(1)} %shard_map.64) | data formatting | bytes 3932160
Async XLA Ops:
  1.4 1.5 %copy-start = (bf16[4,4,160,384]{3,2,1,0:T(8,128)(2,1)S(1)}, bf16[4,4,160,384]{3,2,1,0:T(8,128)(2,1)}, u32[]{:S(2)}) copy-start(bf16[4,4,160,384]{3,2,1,0:T(8,128)(2,1)} %x_ref.1) | copy-start | bytes 5898244
  2.9 0.7 %copy-start.1 = (s32[16]{0:T(128)S(1)}, s32[16]{0:T(128)}, u32[]{:S(2)}) copy-start(s32[16]{0:T(128)} %inter_ref.1) | copy-start | bytes 196
  3.6 0.7 %copy-start.2 = (s32[16]{0:T(128)S(1)}, s32[16]{0:T(128)}, u32[]{:S(2)}) copy-start(s32[16]{0:T(128)} %ramp_ref.1) | copy-start | bytes 196

commit v2 on v1

--- a/solution.py
+++ b/solution.py
@@ -8,7 +8,6 @@
 from jax.sharding import PartitionSpec as P
 
 TAPS = 3
-STEP = 256
 MESH = pl.DeviceIdType.MESH
 
 ROW_OF = ((1, 2), (0, 3))
@@ -16,10 +15,10 @@
 
 def kernel(
     frames, width, chans, count,
-    x_ref, w_ref, gamma_ref, bias_ref, inter_ref, ramp_ref,
+    x_ref, w_ref, gamma_ref, bias_ref, inter_hbm, ramp_hbm,
     out_ref,
-    xbuf, top, bot, lhs, wbuf, acc, ost,
-    xsem, wsem, osem, send_sem, recv_sem,
+    xbuf, top, bot, lhs, wbuf, acc, ost, inter_ref, ramp_ref,
+    xsem, wsem, osem, ssem, send_sem, recv_sem,
 ):
     me = lax.axis_index("rows")
     span = TAPS * chans
@@ -42,6 +41,12 @@
         recv_sem=recv_sem.at[1], device_id={"rows": me - 1}, device_id_type=MESH,
     )
 
+    small = (
+        pltpu.make_async_copy(inter_hbm, inter_ref, ssem.at[0]),
+        pltpu.make_async_copy(ramp_hbm, ramp_ref, ssem.at[1]),
+    )
+    for copy in small:
+        copy.start()
     for f in range(frames):
         x_copy(f).start()
     for t in range(TAPS):
@@ -71,6 +76,9 @@
     @pl.when(me > 0)
     def _():
         up.start()
+
+    for copy in small:
+        copy.wait()
 
     before = jnp.maximum(me - 1, 0)
     prev_ov = jnp.where(me > 0, inter_ref[before], 0)
@@ -83,8 +91,8 @@
     s1 = jnp.where(ovv > 1, 1.0, 1.0 - a0)
     s2 = 1.0 - a1
     live = jnp.where(ownv > 0, 1.0, 0.0)
-    gamma = gamma_ref[...]
-    bias = bias_ref[...]
+    gamma = gamma_ref[...].reshape(1, chans)
+    bias = bias_ref[...].reshape(1, chans)
     columns = lax.broadcasted_iota(jnp.int32, (width, chans), 0)
 
     def activate(values):
@@ -114,31 +122,28 @@
     )
     home = ((1, 0), (0, 0), (0, 1), (1, 1))
 
-    wbuf[:, TAPS * chans :] = jnp.zeros(
-        (wbuf.shape[0], wbuf.shape[1] - TAPS * chans), wbuf.dtype
-    )
-    acc[:, :, frames * chans :] = jnp.zeros(
-        (2, 2 * width, acc.shape[2] - frames * chans), acc.dtype
-    )
-
     def own_frame(f, carry):
         x_copy(f).wait()
-        at = pl.ds(pl.multiple_of(f * chans, 128), chans)
         for row in range(last + 1):
             values = xbuf[f, row].astype(jnp.float32)
             half, slot = home[row]
-            acc[half, slot * width : (slot + 1) * width, at] = values + bias
+            acc[half, f, slot * width : (slot + 1) * width] = values + bias
             place(f, activate(values), own_targets[row])
         return carry
 
     lax.fori_loop(0, frames, own_frame, 0)
 
-    def multiply(half, f, j):
-        taken = pl.ds(pl.multiple_of(j * STEP, STEP), STEP)
-        put = pl.ds(pl.multiple_of(f * chans + j * STEP, 128), STEP)
-        acc[half, :, put] += jnp.dot(
-            lhs[half, f], wbuf[:, taken], preferred_element_type=jnp.float32
-        )
+    def multiply(half, start, stop, t0, t1):
+        block = lhs[half, start:stop].reshape((stop - start) * 2 * width, TAPS * span)
+        product = jnp.dot(
+            block, wbuf[:, t0 * chans : t1 * chans], preferred_element_type=jnp.float32
+        )
+        for f in range(start, stop):
+            for t in range(t0, t1):
+                acc[half, f + t] += product[
+                    (f - start) * 2 * width : (f - start + 1) * 2 * width,
+                    (t - t0) * chans : (t - t0 + 1) * chans,
+                ]
 
     def out_copy(half, f, slot):
         row = ROW_OF[half][slot]
@@ -146,21 +151,21 @@
             ost.at[f, row], out_ref.at[f, row], osem.at[f, row]
         )
 
-    def work(half):
-        for f in range(frames):
-            reach = min(TAPS, frames - f) * chans
-            steps = -(-reach // STEP)
-
-            def body(j, carry, f=f):
-                multiply(half, f, j)
-                return carry
-
-            lax.fori_loop(0, steps, body, 0)
+    def finish(half, start, stop):
+        for f in range(start, stop):
             for slot in range(2):
                 ost[f, ROW_OF[half][slot]] = acc[
-                    half, slot * width : (slot + 1) * width, f * chans : (f + 1) * chans
+                    half, f, slot * width : (slot + 1) * width
                 ].astype(jnp.bfloat16)
                 out_copy(half, f, slot).start()
+
+    def work(half):
+        multiply(half, 0, frames - 1, 0, 2)
+        finish(half, 0, frames - 2)
+        multiply(half, 0, frames - 2, 2, 3)
+        finish(half, frames - 2, frames - 1)
+        multiply(half, frames - 1, frames, 0, 1)
+        finish(half, frames - 1, frames)
 
     for t in range(TAPS):
         w_copy(t).wait()
@@ -209,35 +214,34 @@
     count = lax.axis_size("rows")
     taps = weight.reshape(TAPS, TAPS * TAPS * chans, chans)
     depth = taps.shape[1]
-    wide = -(-TAPS * chans // STEP) * STEP
-    total = (frames - 1) * chans + -(-chans // STEP) * STEP
-    total = max(total, (frames - TAPS) * chans + wide)
-    any_space = pl.BlockSpec(memory_space=pl.ANY)
+    hbm = pl.BlockSpec(memory_space=pltpu.HBM)
     vmem = pl.BlockSpec(memory_space=pltpu.VMEM)
-    smem = pl.BlockSpec(memory_space=pltpu.SMEM)
     return pl.pallas_call(
         functools.partial(kernel, frames, width, chans, count),
         out_shape=jax.ShapeDtypeStruct(latents.shape, latents.dtype),
-        in_specs=[any_space, any_space, vmem, vmem, smem, smem],
-        out_specs=any_space,
+        in_specs=[hbm, hbm, vmem, vmem, hbm, hbm],
+        out_specs=hbm,
         scratch_shapes=[
             pltpu.VMEM((frames, rows, width, chans), jnp.bfloat16),
             pltpu.VMEM((frames, width, chans), jnp.bfloat16),
             pltpu.VMEM((frames, width, chans), jnp.bfloat16),
             pltpu.VMEM((2, frames, 2 * width, depth), jnp.bfloat16),
-            pltpu.VMEM((depth, wide), jnp.bfloat16),
-            pltpu.VMEM((2, 2 * width, total), jnp.float32),
+            pltpu.VMEM((depth, TAPS * chans), jnp.bfloat16),
+            pltpu.VMEM((2, frames, 2 * width, chans), jnp.float32),
             pltpu.VMEM((frames, rows, width, chans), jnp.bfloat16),
+            pltpu.SMEM(intersection.shape, jnp.int32),
+            pltpu.SMEM(ramp.shape, jnp.int32),
             pltpu.SemaphoreType.DMA((frames,)),
             pltpu.SemaphoreType.DMA((TAPS,)),
             pltpu.SemaphoreType.DMA((frames, rows)),
             pltpu.SemaphoreType.DMA((2,)),
             pltpu.SemaphoreType.DMA((2,)),
+            pltpu.SemaphoreType.DMA((2,)),
         ],
         compiler_params=pltpu.CompilerParams(
-            collective_id=0, has_side_effects=True, vmem_limit_bytes=50 * 1024 * 1024
+            collective_id=0, has_side_effects=True, vmem_limit_bytes=64 * 1024 * 1024
         ),
-    )(latents, taps, gamma.reshape(1, chans), bias.reshape(1, chans), intersection, ramp)
+    )(latents, taps, gamma, bias, intersection, ramp)
 
 
 def solution(mesh):

time: 40.3 us -> 30.9 us (0.77)
  Pallas kernels: 34.6 us -> 27.7 us
  local copies, waits for them, and re-layouts: 5.49 us -> 3.02 us
    pallas_call x1, Pallas kernels: 34.6 us -> 27.7 us  [per_device(): pl.pallas_call(functools.partial(kernel, frames, width, chans, count), ou...]
    reshape x2 -> x0, local copies, waits for them, and re-layouts: 1.37 us -> none  [the longest x1 0.68 us: per_device(): gamma.reshape(1, chans)]
    unnamed x7 -> x1, local copies, waits for them, and re-layouts: 4.13 us -> 3.02 us
where the time goes in v2:
time: 30.9 us; the launch traced here: 30.8 us
  Pallas kernels  27.7 us (90%)
  local copies, waits for them, and re-layouts  3.02 us (10%)
    pallas_call x1, Pallas kernels, per_device(): pl.pallas_call(functools.partial(kernel, frames, width, chans, count), ou...  27.7 us
    unnamed x1, local copies, waits for them, and re-layouts  3.02 us

profile of v2, /device:TPU:1, one launch (start us, length us, event | category | flops | bytes accessed | tf_op | source)
XLA Modules:
  0.0 30.8 jit_solution(1198696768369439579)
XLA Ops:
  0.0 27.7 %shard_map.64 = bf16[4,4,160,384]{3,2,1,0:T(8,128)(2,1)} custom-call(bf16[4,4,160,384]{3,2,1,0:T(8,128)(2,1)} %x_ref.1, bf16[3,3456,384]{2,1,0:T(8,128)(2,1)} %bitcast.1, f32[384]{0:T(512)} %gamma_ref.1, f32[384]{0:T(512)} %bias_ref.1, s32[16]{0:T(128)} %inter_hbm.1, s32[16]{0:T(128)} %ramp_hbm.1), custom_call_target="tpu_custom_call" | custom-call | tf_op jit(solution)/shard_map/pallas_call | solution.py:219
  27.7 3.0 %copy.8 = bf16[4,4,160,384]{3,2,1,0:T(8,128)(2,1)} copy(bf16[4,4,160,384]{3,2,1,0:T(8,128)(2,1)} %shard_map.64) | data formatting | bytes 3932160

commit v3 on v2

--- a/solution.py
+++ b/solution.py
@@ -120,18 +120,17 @@
         ((None, ((0, 1, 1), (1, 1, 0))), (s2, ((0, 0, 2),))),
         ((None, ((0, 1, 2), (1, 1, 1))),),
     )
-    home = ((1, 0), (0, 0), (0, 1), (1, 1))
 
     def own_frame(f, carry):
         x_copy(f).wait()
         for row in range(last + 1):
             values = xbuf[f, row].astype(jnp.float32)
-            half, slot = home[row]
-            acc[half, f, slot * width : (slot + 1) * width] = values + bias
             place(f, activate(values), own_targets[row])
         return carry
 
     lax.fori_loop(0, frames, own_frame, 0)
+
+    written = set()
 
     def multiply(half, start, stop, t0, t1):
         block = lhs[half, start:stop].reshape((stop - start) * 2 * width, TAPS * span)
@@ -140,10 +139,15 @@
         )
         for f in range(start, stop):
             for t in range(t0, t1):
-                acc[half, f + t] += product[
+                part = product[
                     (f - start) * 2 * width : (f - start + 1) * 2 * width,
                     (t - t0) * chans : (t - t0 + 1) * chans,
                 ]
+                if (half, f + t) in written:
+                    acc[half, f + t] += part
+                else:
+                    acc[half, f + t] = part
+                    written.add((half, f + t))
 
     def out_copy(half, f, slot):
         row = ROW_OF[half][slot]
@@ -154,9 +158,10 @@
     def finish(half, start, stop):
         for f in range(start, stop):
             for slot in range(2):
-                ost[f, ROW_OF[half][slot]] = acc[
-                    half, f, slot * width : (slot + 1) * width
-                ].astype(jnp.bfloat16)
+                row = ROW_OF[half][slot]
+                total = acc[half, f, slot * width : (slot + 1) * width]
+                total = total + (xbuf[f, row].astype(jnp.float32) + bias)
+                ost[f, row] = total.astype(jnp.bfloat16)
                 out_copy(half, f, slot).start()
 
     def work(half):
@@ -209,6 +214,25 @@
         up.wait_send()
 
 
+def hand_on(frames, rows, from_ref, to_ref, held, in_sem, out_sem):
+    blocks = [(f, r) for f in range(frames) for r in range(rows)]
+    fetch = [
+        pltpu.make_async_copy(from_ref.at[at], held.at[at], in_sem.at[at])
+        for at in blocks
+    ]
+    store = [
+        pltpu.make_async_copy(held.at[at], to_ref.at[at], out_sem.at[at])
+        for at in blocks
+    ]
+    for copy in fetch:
+        copy.start()
+    for arriving, leaving in zip(fetch, store):
+        arriving.wait()
+        leaving.start()
+    for copy in store:
+        copy.wait()
+
+
 def per_device(latents, gamma, weight, bias, intersection, ramp):
     frames, rows, width, chans = latents.shape
     count = lax.axis_size("rows")
@@ -216,7 +240,7 @@
     depth = taps.shape[1]
     hbm = pl.BlockSpec(memory_space=pltpu.HBM)
     vmem = pl.BlockSpec(memory_space=pltpu.VMEM)
-    return pl.pallas_call(
+    made = pl.pallas_call(
         functools.partial(kernel, frames, width, chans, count),
         out_shape=jax.ShapeDtypeStruct(latents.shape, latents.dtype),
         in_specs=[hbm, hbm, vmem, vmem, hbm, hbm],
@@ -242,6 +266,18 @@
             collective_id=0, has_side_effects=True, vmem_limit_bytes=64 * 1024 * 1024
         ),
     )(latents, taps, gamma, bias, intersection, ramp)
+    return pl.pallas_call(
+        functools.partial(hand_on, frames, rows),
+        out_shape=jax.ShapeDtypeStruct(latents.shape, latents.dtype),
+        in_specs=[hbm],
+        out_specs=hbm,
+        scratch_shapes=[
+            pltpu.VMEM((frames, rows, width, chans), jnp.bfloat16),
+            pltpu.SemaphoreType.DMA((frames, rows)),
+            pltpu.SemaphoreType.DMA((frames, rows)),
+        ],
+        compiler_params=pltpu.CompilerParams(vmem_limit_bytes=64 * 1024 * 1024),
+    )(made)
 
 
 def solution(mesh):

time: 30.9 us -> 30.4 us (0.984)
  local copies, waits for them, and re-layouts: 3.02 us -> 0 us
  Pallas kernels: 27.7 us -> 30.1 us
    unnamed x1 -> x0, local copies, waits for them, and re-layouts: 3.02 us -> none
    pallas_call x0 -> x1, Pallas kernels: none -> 2.53 us  [per_device(): pl.pallas_call(functools.partial(hand_on, frames, rows), out_shape=jax.Sh...]
where the time goes in v3:
time: 30.4 us; the launch traced here: 30.2 us
  Pallas kernels  30.1 us (99%)
    pallas_call x1, Pallas kernels, per_device(): pl.pallas_call(functools.partial(kernel, frames, width, chans, count), ou...  27.5 us
    pallas_call x1, Pallas kernels, per_device(): pl.pallas_call(functools.partial(hand_on, frames, rows), out_shape=jax.Sh...  2.53 us

profile of v3, /device:TPU:1, one launch (start us, length us, event | category | flops | bytes accessed | tf_op | source)
XLA Modules:
  0.0 30.2 jit_solution(7899431851345634215)
XLA Ops:
  0.0 27.5 %shard_map.64.from_ref = bf16[4,4,160,384]{3,2,1,0:T(8,128)(2,1)} custom-call(bf16[4,4,160,384]{3,2,1,0:T(8,128)(2,1)} %x_ref.1, bf16[3,3456,384]{2,1,0:T(8,128)(2,1)} %bitcast.1, f32[384]{0:T(512)} %gamma_ref.1, f32[384]{0:T(512)} %bias_ref.1, s32[16]{0:T(128)} %inter_hbm.1, s32[16]{0:T(128)} %ramp_hbm.1), custom_call_target="tpu_custom_call" | custom-call | tf_op jit(solution)/shard_map/pallas_call | solution.py:243
  27.5 2.5 %shard_map.65 = bf16[4,4,160,384]{3,2,1,0:T(8,128)(2,1)} custom-call(bf16[4,4,160,384]{3,2,1,0:T(8,128)(2,1)} %shard_map.64.from_ref), custom_call_target="tpu_custom_call" | custom-call | tf_op jit(solution)/shard_map/pallas_call | solution.py:269
